TPU v7x, 32 devices: a whole 2x2x4 slice. The times are simulated.
32 devices in a mesh: dp: 4 (over z), fsdp: 8 (over y, x, core).
Axes of the slice: x: 2, y: 2, z: 4, core: 2. Of those that a mesh axis runs over, the one named last changes fastest.
Arguments:
- tokens: bfloat16 [128, 8192], P('dp', 'fsdp'), may hold values from -6 to 6
- cotangent: bfloat16 [128, 8192], P('dp', 'fsdp'), may hold values from -6 to 6
- w_gate: bfloat16 [16384, 8192], P(('dp', 'fsdp')), may hold values from -0.0625 to 0.0625
- w_up: bfloat16 [16384, 8192], P(('dp', 'fsdp')), may hold values from -0.0625 to 0.0625
- w_down: bfloat16 [16384, 8192], P(('dp', 'fsdp')), may hold values from -0.046875 to 0.046875
- t_gate: bfloat16 [16384, 8192], P(('dp', 'fsdp')), may hold values from -0.0625 to 0.0625
- t_up: bfloat16 [16384, 8192], P(('dp', 'fsdp')), may hold values from -0.0625 to 0.0625
Outputs:
- hvp_gate: float32 [16384, 8192], P(('dp', 'fsdp'))
- hvp_up: float32 [16384, 8192], P(('dp', 'fsdp'))
All inputs are finite; a program needn't handle non-finite values.
Results may differ from a plain program's by a relative error of at most 0.003.
Values may be sent and summed in bfloat16 or wider, within the bound.
A program may use at most 192 MiB of HBM per device.

v0:
```python
import math

import jax
import jax.numpy as jnp
from jax import lax
from jax.sharding import PartitionSpec as P


def contract(weight, block):
    return lax.dot_general(
        weight, block, (((1,), (1,)), ((), ())), preferred_element_type=jnp.float32
    )


def local_terms(block_tok, block_cot, weights):
    w_gate, w_up, w_down, t_gate, t_up = weights
    gate = contract(w_gate, block_tok)
    up = contract(w_up, block_tok)
    gate_dot = contract(t_gate, block_tok)
    up_dot = contract(t_up, block_tok)
    back = contract(w_down, block_cot)
    sigmoid_gate = jax.nn.sigmoid(gate)
    first = sigmoid_gate * (1.0 + gate * (1.0 - sigmoid_gate))
    second = sigmoid_gate * (1.0 - sigmoid_gate) * (2.0 + gate * (1.0 - 2.0 * sigmoid_gate))
    factor_gate = (back * (up_dot * first + up * second * gate_dot)).astype(jnp.bfloat16)
    factor_up = (back * first * gate_dot).astype(jnp.bfloat16)
    term_gate = jnp.dot(factor_gate, block_tok, preferred_element_type=jnp.float32)
    term_up = jnp.dot(factor_up, block_tok, preferred_element_type=jnp.float32)
    return (term_gate, term_up)


def local(tokens, cotangent, w_gate, w_up, w_down, t_gate, t_up):
    weights = (w_gate, w_up, w_down, t_gate, t_up)
    scale = 1.0 / math.sqrt(tokens.shape[0] * lax.axis_size("dp"))
    full_tok, full_cot = (
        lax.all_gather(tokens, "fsdp", axis=1, tiled=True),
        lax.all_gather(cotangent, "fsdp", axis=1, tiled=True),
    )
    term_gate, term_up = local_terms(
        lax.all_gather(full_tok, "dp", axis=0, tiled=True),
        lax.all_gather(full_cot, "dp", axis=0, tiled=True),
        weights,
    )
    return (term_gate * scale, term_up * scale)


def solution(mesh):
    in_specs = (
        P("dp", "fsdp"),
        P("dp", "fsdp"),
        P(("dp", "fsdp"), None),
        P(("dp", "fsdp"), None),
        P(("dp", "fsdp"), None),
        P(("dp", "fsdp"), None),
        P(("dp", "fsdp"), None),
    )
    out_specs = (P(("dp", "fsdp"), None), P(("dp", "fsdp"), None))
    return jax.shard_map(local, mesh=mesh, in_specs=in_specs, out_specs=out_specs, check_vma=False)
```

profile of v0, /device:TPU:0, one launch (start us, length us, event | category | flops | bytes accessed | tf_op | source)
XLA Modules:
  0.0 155.2 jit_solution(3539089136622723190)
XLA Ops:
  7.2 0.0 all-gather.5.cloned.1.call-start
  7.2 13.3 %all_gather.14 = bf16[32,8192]{1,0:T(8,128)(2,1)} all-gather(bf16[32,1024]{1,0:T(8,128)(2,1)} %param.7), channel_id=1, replica_groups=mesh['dp'=4,'fsdp'=8] {'fsdp'}, dimensions={1}, use_global_device_ids=true | all-gather | bytes 589824 | tf_op jit(solution)/shard_map/all_gather | solution.py:36
  20.5 0.0 all-gather.5.cloned.1.call-update
  20.5 0.0 all-gather.3.cloned.1.call-start
  20.5 10.8 %all_gather.12 = bf16[32,8192]{1,0:T(8,128)(2,1)} all-gather(bf16[32,1024]{1,0:T(8,128)(2,1)} %param.8), channel_id=1, replica_groups=mesh['dp'=4,'fsdp'=8] {'fsdp'}, dimensions={1}, use_global_device_ids=true | all-gather | bytes 589824 | tf_op jit(solution)/shard_map/all_gather | solution.py:37
  31.4 0.0 all-gather.3.cloned.1.call-update
  31.4 35.5 %all-gather.5.cloned.1.call-done = bf16[128,8192]{1,0:T(8,128)(2,1)} async-done(((bf16[32,8192]{1,0:T(8,128)(2,1)}), bf16[128,8192]{1,0:T(8,128)(2,1)}) %all-gather.5.cloned.1.call-update) | async-done | bytes 2097168 | tf_op jit(solution)/shard_map/all_gather | solution.py:40
  66.9 0.0 copy-start
  66.9 0.0 copy-start.1
  66.9 6.5 %fusion.10 = f32[512,128]{1,0:T(8,128)S(1)} fusion(bf16[512,8192]{1,0:T(8,128)(2,1)} %param.9, bf16[128,8192]{1,0:T(8,128)(2,1)} %all-gather.5.cloned.1.call-done), kind=kOutput, calls=%fused_computation.16 | convolution fusion | flops 1073741824 | bytes 10747904 | tf_op jit(solution)/shard_map/dot_general | solution.py:10
  73.4 0.0 copy-done
  73.4 0.6 copy-done.1
  74.0 2.3 %fusion.11 = f32[512,128]{1,0:T(8,128)S(1)} fusion(bf16[512,8192]{1,0:T(8,128)(2,1)S(1)} %copy-done.1, bf16[128,8192]{1,0:T(8,128)(2,1)S(1)} %copy-done), kind=kOutput, calls=%fused_computation.17 | convolution fusion | flops 1073741824 | bytes 10747904 | tf_op jit(solution)/shard_map/dot_general | solution.py:10
  76.3 36.9 %all-gather.3.cloned.1.call-done = bf16[128,8192]{1,0:T(8,128)(2,1)} async-done(((bf16[32,8192]{1,0:T(8,128)(2,1)}), bf16[128,8192]{1,0:T(8,128)(2,1)}) %all-gather.3.cloned.1.call-update) | async-done | bytes 2097168 | tf_op jit(solution)/shard_map/all_gather | solution.py:41
  113.1 6.3 %fusion.9 = f32[512,128]{1,0:T(8,128)S(1)} fusion(bf16[512,8192]{1,0:T(8,128)(2,1)} %param.11, bf16[128,8192]{1,0:T(8,128)(2,1)} %all-gather.3.cloned.1.call-done), kind=kOutput, calls=%fused_computation.15 | convolution fusion | flops 1073741824 | bytes 10747904 | tf_op jit(solution)/shard_map/dot_general | solution.py:10
  119.5 5.7 %fusion = f32[512,128]{1,0:T(8,128)S(1)} fusion(f32[512,128]{1,0:T(8,128)S(1)} %fusion.11, bf16[512,8192]{1,0:T(8,128)(2,1)} %param.10, bf16[128,8192]{1,0:T(8,128)(2,1)S(1)} %copy-done, f32[512,128]{1,0:T(8,128)S(1)} %fusion.10), kind=kOutput, calls=%fused_computation.3 | convolution fusion | flops 1074528256 | bytes 11272192 | tf_op jit(solution)/shard_map/dot_general | solution.py:10
  125.2 8.5 %convolution_multiply_fusion = f32[512,8192]{1,0:T(8,128)} fusion(bf16[128,8192]{1,0:T(8,128)(2,1)S(1)} %copy-done, f32[512,128]{1,0:T(8,128)S(1)} %fusion.11, f32[512,128]{1,0:T(8,128)S(1)} %fusion.9, f32[512,128]{1,0:T(8,128)S(1)} %fusion.10), kind=kOutput, calls=%fused_computation | convolution fusion | flops 1078591488 | bytes 19660800 | tf_op jit(solution)/shard_map/dot_general | solution.py:28
  133.7 14.7 %convolution_multiply_fusion.1 = f32[512,8192]{1,0:T(8,128)} fusion(bf16[128,8192]{1,0:T(8,128)(2,1)S(1)} %copy-done, f32[512,128]{1,0:T(8,128)S(1)} %fusion.9, f32[512,128]{1,0:T(8,128)S(1)} %fusion, bf16[512,8192]{1,0:T(8,128)(2,1)} %param.13, f32[512,128]{1,0:T(8,128)S(1)} %fusion.10), kind=kOutput, calls=%fused_computation.1 | convolution fusion | flops 2152398848 | bytes 28049408 | tf_op jit(solution)/shard_map/dot_general | solution.py:27
Async XLA Ops:
  7.2 59.7 %all-gather.5.cloned.1.call-start = ((), (), s32[]{:S(2)}) async-start(), calls=%async_computation.1 | async-start | bytes 2621440 | tf_op jit(solution)/shard_map/all_gather | solution.py:40
  20.5 92.6 %all-gather.3.cloned.1.call-start = ((), (), s32[]{:S(2)}) async-start(), calls=%async_computation | async-start | bytes 2621440 | tf_op jit(solution)/shard_map/all_gather | solution.py:41
  66.9 6.5 %copy-start = (bf16[128,8192]{1,0:T(8,128)(2,1)S(1)}, bf16[128,8192]{1,0:T(8,128)(2,1)}, u32[]{:S(2)}) copy-start(bf16[128,8192]{1,0:T(8,128)(2,1)} %all-gather.5.cloned.1.call-done) | copy-start | bytes 6291460
  66.9 7.1 %copy-start.1 = (bf16[512,8192]{1,0:T(8,128)(2,1)S(1)}, bf16[512,8192]{1,0:T(8,128)(2,1)}, u32[]{:S(2)}) copy-start(bf16[512,8192]{1,0:T(8,128)(2,1)} %param.12) | copy-start | bytes 25165828
Sparse Core Ops, SparseCore 0:
  20.6 46.2 all-gather.4
  68.5 44.6 all-gather.2
where the time goes:
time: 155 us
  waiting for transfers between devices  72.4 us (47%)
  matrix products  44 us (28%)
  blocking collectives  24.1 us (16%)
  between operations  14.1 us (9%)
    all_gather x1, waiting for transfers between devices, local(): lax.all_gather(full_cot, 'dp', axis=0, tiled=True)  36.9 us
    all_gather x1, waiting for transfers between devices, local(): lax.all_gather(full_tok, 'dp', axis=0, tiled=True)  35.5 us
    dot_general x4, matrix products, contract(): lax.dot_general(weight, block, (((1,), (1,)), ((), ())), preferred_elemen...  20.8 us
    dot_general x1, matrix products, local_terms(): jnp.dot(factor_gate, block_tok, preferred_element_type=jnp.float32)  14.7 us
    all_gather x1, blocking collectives, local(): lax.all_gather(tokens, 'fsdp', axis=1, tiled=True)  13.3 us
    all_gather x1, blocking collectives, local(): lax.all_gather(cotangent, 'fsdp', axis=1, tiled=True)  10.8 us
    dot_general x1, matrix products, local_terms(): term_up = jnp.dot(factor_up, block_tok, preferred_element_type=jnp.float32)  8.51 us
  transfers between devices with their start and end apart: 2, of which 2 were waited for; matrix products, arithmetic and copies ran while one was open for 6% of the time, Pallas kernels for 0%

commit v1 on v0

v1 whole, which is shorter than its diff:
```python
import functools
import math

import jax
import jax.numpy as jnp
from jax import lax
from jax.experimental import pallas as pl
from jax.experimental.pallas import tpu as pltpu
from jax.sharding import PartitionSpec as P

MESH = pl.DeviceIdType.MESH


def contract(weight, block):
    return lax.dot_general(
        weight, block, (((1,), (1,)), ((), ())), preferred_element_type=jnp.float32
    )


def factors(gate, up, gate_dot, up_dot, back):
    s = jax.nn.sigmoid(gate)
    first = s * (1.0 + gate * (1.0 - s))
    second = s * (1.0 - s) * (2.0 + gate * (1.0 - 2.0 * s))
    factor_gate = (back * (up_dot * first + up * second * gate_dot)).astype(jnp.bfloat16)
    factor_up = (back * first * gate_dot).astype(jnp.bfloat16)
    return factor_gate, factor_up


def gather_kernel(
    tok_hbm, cot_hbm, wg, wu, tg, tu, wd,
    fg_out, fu_out, tok_out,
    w4, wdn, buf, acc, accb,
    wsem, dsem, isem, osem,
    zs, zr, xs, xr, ys, yr, dxs, dxr, dys, dyr, ss, sr,
):
    rows, cols = tok_hbm.shape
    hidden = wg.shape[0]
    half = rows // 2
    z = lax.axis_index("dp")
    f = lax.axis_index("fsdp")
    core = f % 2
    q = f // 2
    x = q % 2
    y = q // 2

    def feat(yy, xx, cc):
        return (yy * 2 + xx) * 2 + cc

    fx = feat(y, 1 - x, core)
    fy = feat(1 - y, x, core)
    fs = feat(y, x, 1 - core)
    fidx = [feat(yy, xx, cc) for cc in (core, 1 - core)
            for yy, xx in ((y, x), (y, 1 - x), (1 - y, x), (1 - y, 1 - x))]
    zi = [z, z + 1 - 2 * (z % 2), (z + 2) % 4, 3 - z]

    inputs = [pltpu.make_async_copy(src, buf.at[t, 0, pl.ds(0, rows)], isem.at[t])
              for t, src in enumerate((tok_hbm, cot_hbm))]
    for c in inputs:
        c.start()

    barrier = pltpu.get_barrier_semaphore()
    partners = [(zi[1], f), (zi[2], f), (zi[3], f), (z, fx), (z, fy), (z, fs)]
    for who in partners:
        pl.semaphore_signal(barrier, inc=1, device_id=who, device_id_type=MESH)

    loads = []
    for p in range(8):
        loads.append([
            pltpu.make_async_copy(
                src.at[:, pl.ds(pl.multiple_of(fidx[p] * cols, cols), cols)],
                w4.at[p, pl.ds(w * hidden, hidden)], wsem.at[p, w])
            for w, src in enumerate((wg, wu, tg, tu))])
    dloads = [
        pltpu.make_async_copy(
            wd.at[:, pl.ds(pl.multiple_of(fidx[p] * cols, cols), cols)],
            wdn.at[p], dsem.at[p])
        for p in range(8)]
    for group in loads:
        for c in group:
            c.start()
    for c in dloads:
        c.start()

    def remote(t, p_src, p_dst, r_src, r_dst, n, send, recv, who):
        return pltpu.make_async_remote_copy(
            src_ref=buf.at[t, p_src, pl.ds(r_src, n)],
            dst_ref=buf.at[t, p_dst, pl.ds(r_dst, n)],
            send_sem=send, recv_sem=recv, device_id=who, device_id_type=MESH)

    def zcopy(t, i):
        return remote(t, 0, 0, 0, i * rows, rows, zs.at[t, i], zr.at[t, i], (zi[i], f))

    def xcopy(t, i):
        return remote(t, 0, 1, i * rows, i * rows, rows, xs.at[t, i], xr.at[t, i], (z, fx))

    def ycopy(t, i):
        return remote(t, 0, 2, i * rows, i * rows, rows, ys.at[t, i], yr.at[t, i], (z, fy))

    def dycopy(t, i):
        return remote(t, 1, 3, i * rows, i * rows, half, dys.at[t, i], dyr.at[t, i], (z, fy))

    def dxcopy(t, i):
        r = i * rows + half
        return remote(t, 2, 3, r, r, half, dxs.at[t, i], dxr.at[t, i], (z, fx))

    def scopy(t, p, h):
        r = h * 2 * rows
        return remote(t, p, 4 + p, r, r, 2 * rows, ss.at[t, p, h], sr.at[t, p, h], (z, fs))

    def own_z(t):
        for i in (1, 2, 3):
            zcopy(t, i).start()

    def own_xy(t):
        xcopy(t, 0).start()
        ycopy(t, 0).start()

    def pass_z(t, i):
        zcopy(t, i).wait_recv()
        xcopy(t, i).start()
        ycopy(t, i).start()
        if i % 2 == 1:
            scopy(t, 0, i // 2).start()

    def pass_xy(t, i):
        xcopy(t, i).wait_recv()
        dycopy(t, i).start()
        ycopy(t, i).wait_recv()
        dxcopy(t, i).start()
        if i % 2 == 1:
            scopy(t, 1, i // 2).start()
            scopy(t, 2, i // 2).start()

    def pass_d(t, h):
        for i in (2 * h, 2 * h + 1):
            dycopy(t, i).wait_recv()
            dxcopy(t, i).wait_recv()
        scopy(t, 3, h).start()

    def ready_sib(t, p):
        if p >= 4:
            scopy(t, p - 4, 0).wait_recv()
            scopy(t, p - 4, 1).wait_recv()

    out_copies = [pltpu.make_async_copy(buf.at[0, p], tok_out.at[fidx[p]], osem.at[p])
                  for p in range(8)]

    def dots(p, part):
        for w in (2 * part, 2 * part + 1):
            loads[p][w].wait()

        def body(k, carry):
            r = pl.ds(pl.multiple_of(k * hidden, hidden), hidden)
            d = contract(w4[p, r], buf[0, p])
            if p == 0:
                acc[r] = d
            else:
                acc[r] += d
            return carry
        lax.fori_loop(2 * part, 2 * part + 2, body, 0)

    for c in inputs:
        c.wait()
    pl.semaphore_wait(barrier, len(partners))

    own_z(0)
    own_xy(0)
    pass_z(0, 1)
    pass_xy(0, 0)
    pass_z(0, 2)
    pass_xy(0, 1)
    pass_z(0, 3)
    own_z(1)
    pass_d(0, 0)
    pass_xy(0, 2)
    own_xy(1)
    pass_xy(0, 3)
    pass_d(0, 1)

    def step(p, first=None, second=None):
        ready_sib(0, p)
        out_copies[p].start()
        dots(p, 0)
        if first is not None:
            first()
        dots(p, 1)
        if second is not None:
            second()

    step(0, lambda: pass_z(1, 1))
    step(1, lambda: pass_xy(1, 0))
    step(2, lambda: pass_z(1, 2))
    step(3, lambda: pass_xy(1, 1), lambda: pass_z(1, 3))
    step(4, lambda: pass_d(1, 0))
    step(5, lambda: pass_xy(1, 2))
    step(6)
    step(7, lambda: pass_xy(1, 3))


    def back(p):
        ready_sib(1, p)
        dloads[p].wait()
        d = contract(wdn[p], buf[1, p])
        if p == 0:
            accb[...] = d
        else:
            accb[...] += d

    back(0)
    pass_d(1, 1)
    for p in (1, 2, 3, 4, 5, 6, 7):
        back(p)

    chunk = hidden // 4

    def finish(k, carry):
        def part(w):
            return acc[pl.ds(pl.multiple_of(w * hidden + k * chunk, chunk), chunk)]
        r = pl.ds(pl.multiple_of(k * chunk, chunk), chunk)
        fg, fu = factors(part(0), part(1), part(2), part(3), accb[r])
        fg_out[r] = fg
        fu_out[r] = fu
        return carry
    lax.fori_loop(0, 4, finish, 0)

    for c in out_copies:
        c.wait()
    for t in (0, 1):
        for i in (1, 2, 3):
            zcopy(t, i).wait_send()
        for i in range(4):
            xcopy(t, i).wait_send()
            ycopy(t, i).wait_send()
            dxcopy(t, i).wait_send()
            dycopy(t, i).wait_send()
        for p in range(4):
            for h in (0, 1):
                scopy(t, p, h).wait_send()


def outer_kernel(scale, fg, fu, tok, og, ou):
    t = tok[0]
    og[...] = jnp.dot(fg[...], t, preferred_element_type=jnp.float32) * scale
    ou[...] = jnp.dot(fu[...], t, preferred_element_type=jnp.float32) * scale


def local_kernels(tokens, cotangent, w_gate, w_up, w_down, t_gate, t_up):
    n_dp, n_fs = lax.axis_size("dp"), lax.axis_size("fsdp")
    rows, cols = tokens.shape
    hidden, width = w_gate.shape
    total = rows * n_dp
    scale = 1.0 / math.sqrt(total)
    anywhere = pl.BlockSpec(memory_space=pl.ANY)
    vmem = pl.BlockSpec(memory_space=pltpu.VMEM)
    dma = pltpu.SemaphoreType.DMA
    fg, fu, tok = pl.pallas_call(
        gather_kernel,
        out_shape=(
            jax.ShapeDtypeStruct((hidden, total), jnp.bfloat16),
            jax.ShapeDtypeStruct((hidden, total), jnp.bfloat16),
            jax.ShapeDtypeStruct((n_fs, total, cols), jnp.bfloat16),
        ),
        in_specs=[anywhere] * 7,
        out_specs=(vmem, vmem, anywhere),
        scratch_shapes=[
            pltpu.VMEM((n_fs, 4 * hidden, cols), jnp.bfloat16),
            pltpu.VMEM((n_fs, hidden, cols), jnp.bfloat16),
            pltpu.VMEM((2, n_fs, total, cols), jnp.bfloat16),
            pltpu.VMEM((4 * hidden, total), jnp.float32),
            pltpu.VMEM((hidden, total), jnp.float32),
            dma((8, 4)), dma((8,)), dma((2,)), dma((8,)),
        ] + [dma((2, 4))] * 10 + [dma((2, 4, 2))] * 2,
        compiler_params=pltpu.CompilerParams(
            collective_id=0, has_side_effects=True, vmem_limit_bytes=56 * 2**20),
        cost_estimate=pl.CostEstimate(
            flops=10 * hidden * width * total, bytes_accessed=10 * hidden * width,
            transcendentals=hidden * total),
        name="gather_factors",
    )(tokens, cotangent, w_gate, w_up, t_gate, t_up, w_down)
    whole = pl.BlockSpec((hidden, total), lambda j: (0, 0))
    out = pl.BlockSpec((hidden, cols), lambda j: (0, j))
    return pl.pallas_call(
        functools.partial(outer_kernel, scale),
        grid=(n_fs,),
        out_shape=(jax.ShapeDtypeStruct((hidden, width), jnp.float32),) * 2,
        in_specs=[whole, whole, pl.BlockSpec((1, total, cols), lambda j: (j, 0, 0))],
        out_specs=(out, out),
        compiler_params=pltpu.CompilerParams(vmem_limit_bytes=32 * 2**20),
        cost_estimate=pl.CostEstimate(
            flops=4 * hidden * width * total, bytes_accessed=8 * hidden * width,
            transcendentals=0),
        name="outer",
    )(fg, fu, tok)


def local(tokens, cotangent, w_gate, w_up, w_down, t_gate, t_up):
    scale = 1.0 / math.sqrt(tokens.shape[0] * lax.axis_size("dp"))
    full_tok, full_cot = (
        lax.all_gather(lax.all_gather(a, "fsdp", axis=1, tiled=True), "dp", axis=0, tiled=True)
        for a in (tokens, cotangent)
    )
    factor_gate, factor_up = factors(
        *(contract(w, full_tok) for w in (w_gate, w_up, t_gate, t_up)),
        contract(w_down, full_cot),
    )
    return tuple(
        jnp.dot(a, full_tok, preferred_element_type=jnp.float32) * scale
        for a in (factor_gate, factor_up)
    )


def solution(mesh):
    spec = P("dp", "fsdp")
    weight = P(("dp", "fsdp"), None)
    square = mesh.shape["dp"] == 4 and mesh.shape["fsdp"] == 8
    return jax.shard_map(
        local_kernels if square else local, mesh=mesh,
        in_specs=(spec,) * 2 + (weight,) * 5, out_specs=(weight,) * 2, check_vma=False)
```

time: 155 us -> 59.8 us (0.39)
  waiting for transfers between devices: 72.4 us -> 0 us
  Pallas kernels: 0 us -> 55.5 us
  matrix products: 44 us -> 0 us
  blocking collectives: 24.1 us -> 0 us
  between operations: 14.1 us -> 0.65 us
  local copies, waits for them, and re-layouts: 0.59 us -> 3.39 us
    all_gather x2 -> x0, waiting for transfers between devices: 72.3 us -> none  [the longest x1 36.9 us: local(): lax.all_gather(full_cot, 'dp', axis=0, tiled=True)]
    pallas_call x0 -> x2, Pallas kernels: none -> 55.5 us  [the longest x1 44.2 us: local_kernels(): pl.pallas_call(gather_kernel, out_shape=(jax.ShapeDtypeStruct((hidden, to...]
    dot_general x6 -> x0, matrix products: 44 us -> none  [the longest x4 20.8 us: contract(): lax.dot_general(weight, block, (((1,), (1,)), ((), ())), preferred_elemen...]
    all_gather x2 -> x0, blocking collectives: 24.1 us -> none  [the longest x1 13.3 us: local(): lax.all_gather(tokens, 'fsdp', axis=1, tiled=True)]
    unnamed x4 -> x6, local copies, waits for them, and re-layouts: 0.59 us -> 3.39 us
  transfers between devices with their start and end apart: 2 -> 0, of which waited for: 2 -> 0; matrix products, arithmetic and copies ran while one was open for 6% -> 0% of each run, Pallas kernels for 0% -> 0%
where the time goes in v1:
time: 59.8 us; the launch traced here: 59.6 us
  Pallas kernels  55.5 us (93%)
  local copies, waits for them, and re-layouts  3.39 us (6%)
  between operations  0.65 us (1%)
    pallas_call x1, Pallas kernels, local_kernels(): pl.pallas_call(gather_kernel, out_shape=(jax.ShapeDtypeStruct((hidden, to...  44.2 us
    pallas_call x1, Pallas kernels, local_kernels(): pl.pallas_call(functools.partial(outer_kernel, scale), grid=(n_fs,), out_...  11.3 us
    unnamed x6, local copies, waits for them, and re-layouts  3.39 us

profile of v1, /device:TPU:0, one launch (start us, length us, event | category | flops | bytes accessed | tf_op | source)
XLA Modules:
  0.0 59.6 jit_solution(15072041081473488429)
XLA Ops:
  0.6 44.2 %gather_factors.1 = (bf16[512,128]{1,0:T(8,128)(2,1)}, bf16[512,128]{1,0:T(8,128)(2,1)}, bf16[8,128,1024]{2,1,0:T(8,128)(2,1)}) custom-call(bf16[32,1024]{1,0:T(8,128)(2,1)} %tok_hbm.1, bf16[32,1024]{1,0:T(8,128)(2,1)} %cot_hbm.1, bf16[512,8192]{1,0:T(8,128)(2,1)} %wg.1, bf16[512,8192]{1,0:T(8,128)(2,1)} %wu.1, bf16[512,8192]{1,0:T(8,128)(2,1)} %tg.1, ...), custom_call_target="tpu_custom_call" | custom-call | flops 5368709120 | bytes 41943040 | tf_op jit(solution)/shard_map/gather_factors/pallas_call | solution.py:256
  44.8 0.0 copy-start
  44.9 1.6 %copy-done = bf16[8,128,1024]{2,1,0:T(8,128)(2,1)S(1)} copy-done((bf16[8,128,1024]{2,1,0:T(8,128)(2,1)S(1)}, bf16[8,128,1024]{2,1,0:T(8,128)(2,1)}, u32[]{:S(2)}) %copy-start) | copy-done | bytes 2097176
  46.4 0.0 copy-start.1
  46.4 0.9 %copy-done.1 = bf16[512,128]{1,0:T(8,128)(2,1)S(1)} copy-done((bf16[512,128]{1,0:T(8,128)(2,1)S(1)}, bf16[512,128]{1,0:T(8,128)(2,1)}, u32[]{:S(2)}) %copy-start.1) | copy-done | bytes 131096
  47.3 0.0 copy-start.2
  47.3 0.9 %copy-done.2 = bf16[512,128]{1,0:T(8,128)(2,1)S(1)} copy-done((bf16[512,128]{1,0:T(8,128)(2,1)S(1)}, bf16[512,128]{1,0:T(8,128)(2,1)}, u32[]{:S(2)}) %copy-start.2) | copy-done | bytes 131096
  48.3 11.3 %outer.1 = (f32[512,8192]{1,0:T(8,128)}, f32[512,8192]{1,0:T(8,128)}) custom-call(bf16[512,128]{1,0:T(8,128)(2,1)S(1)} %copy-done.1, bf16[512,128]{1,0:T(8,128)(2,1)S(1)} %copy-done.2, bf16[8,128,1024]{2,1,0:T(8,128)(2,1)S(1)} %copy-done), custom_call_target="tpu_custom_call" | custom-call | flops 2147483648 | bytes 33554432 | tf_op jit(solution)/shard_map/outer/pallas_call | solution.py:282
Async XLA Ops:
  44.8 1.6 %copy-start = (bf16[8,128,1024]{2,1,0:T(8,128)(2,1)S(1)}, bf16[8,128,1024]{2,1,0:T(8,128)(2,1)}, u32[]{:S(2)}) copy-start(bf16[8,128,1024]{2,1,0:T(8,128)(2,1)} %get-tuple-element.7.tok) | copy-start | bytes 6291460
  46.4 0.9 %copy-start.1 = (bf16[512,128]{1,0:T(8,128)(2,1)S(1)}, bf16[512,128]{1,0:T(8,128)(2,1)}, u32[]{:S(2)}) copy-start(bf16[512,128]{1,0:T(8,128)(2,1)} %get-tuple-element.5.fg) | copy-start | bytes 393220
  47.3 0.9 %copy-start.2 = (bf16[512,128]{1,0:T(8,128)(2,1)S(1)}, bf16[512,128]{1,0:T(8,128)(2,1)}, u32[]{:S(2)}) copy-start(bf16[512,128]{1,0:T(8,128)(2,1)} %get-tuple-element.6.fu) | copy-start | bytes 393220

commit v2 on v1

--- a/solution.py
+++ b/solution.py
@@ -48,6 +48,7 @@
 
     fx = feat(y, 1 - x, core)
     fy = feat(1 - y, x, core)
+    fd = feat(1 - y, 1 - x, core)
     fs = feat(y, x, 1 - core)
     fidx = [feat(yy, xx, cc) for cc in (core, 1 - core)
             for yy, xx in ((y, x), (y, 1 - x), (1 - y, x), (1 - y, 1 - x))]
@@ -59,7 +60,7 @@
         c.start()
 
     barrier = pltpu.get_barrier_semaphore()
-    partners = [(zi[1], f), (zi[2], f), (zi[3], f), (z, fx), (z, fy), (z, fs)]
+    partners = [(zi[1], f), (zi[2], f), (zi[3], f), (z, fx), (z, fy), (z, fd), (z, fs)]
     for who in partners:
         pl.semaphore_signal(barrier, inc=1, device_id=who, device_id_type=MESH)
 
@@ -75,11 +76,12 @@
             wd.at[:, pl.ds(pl.multiple_of(fidx[p] * cols, cols), cols)],
             wdn.at[p], dsem.at[p])
         for p in range(8)]
-    for group in loads:
-        for c in group:
+    order = (0, 4, 1, 2, 5, 6, 3, 7)
+    for p in order:
+        for c in loads[p]:
             c.start()
-    for c in dloads:
-        c.start()
+    for p in order:
+        dloads[p].start()
 
     def remote(t, p_src, p_dst, r_src, r_dst, n, send, recv, who):
         return pltpu.make_async_remote_copy(
@@ -103,24 +105,29 @@
         r = i * rows + half
         return remote(t, 2, 3, r, r, half, dxs.at[t, i], dxr.at[t, i], (z, fx))
 
+    def dcopy(i):
+        return remote(1, 0, 3, i * rows, i * rows, rows, dxs.at[1, i], dxr.at[1, i], (z, fd))
+
     def scopy(t, p, h):
         r = h * 2 * rows
         return remote(t, p, 4 + p, r, r, 2 * rows, ss.at[t, p, h], sr.at[t, p, h], (z, fs))
 
-    def own_z(t):
-        for i in (1, 2, 3):
-            zcopy(t, i).start()
-
-    def own_xy(t):
-        xcopy(t, 0).start()
-        ycopy(t, 0).start()
+    def across(t, i):
+        xcopy(t, i).start()
+        ycopy(t, i).start()
+        if t == 1:
+            dcopy(i).start()
 
     def pass_z(t, i):
         zcopy(t, i).wait_recv()
-        xcopy(t, i).start()
-        ycopy(t, i).start()
+        across(t, i)
         if i % 2 == 1:
             scopy(t, 0, i // 2).start()
+
+    def sib(p, h):
+        for i in (2 * h, 2 * h + 1):
+            {1: lambda: xcopy(1, i), 2: lambda: ycopy(1, i), 3: lambda: dcopy(i)}[p]().wait_recv()
+        scopy(1, p, h).start()
 
     def pass_xy(t, i):
         xcopy(t, i).wait_recv()
@@ -145,57 +152,16 @@
     out_copies = [pltpu.make_async_copy(buf.at[0, p], tok_out.at[fidx[p]], osem.at[p])
                   for p in range(8)]
 
-    def dots(p, part):
-        for w in (2 * part, 2 * part + 1):
-            loads[p][w].wait()
-
-        def body(k, carry):
-            r = pl.ds(pl.multiple_of(k * hidden, hidden), hidden)
-            d = contract(w4[p, r], buf[0, p])
-            if p == 0:
-                acc[r] = d
-            else:
-                acc[r] += d
-            return carry
-        lax.fori_loop(2 * part, 2 * part + 2, body, 0)
-
-    for c in inputs:
-        c.wait()
-    pl.semaphore_wait(barrier, len(partners))
-
-    own_z(0)
-    own_xy(0)
-    pass_z(0, 1)
-    pass_xy(0, 0)
-    pass_z(0, 2)
-    pass_xy(0, 1)
-    pass_z(0, 3)
-    own_z(1)
-    pass_d(0, 0)
-    pass_xy(0, 2)
-    own_xy(1)
-    pass_xy(0, 3)
-    pass_d(0, 1)
-
-    def step(p, first=None, second=None):
+    def step(p):
         ready_sib(0, p)
         out_copies[p].start()
-        dots(p, 0)
-        if first is not None:
-            first()
-        dots(p, 1)
-        if second is not None:
-            second()
-
-    step(0, lambda: pass_z(1, 1))
-    step(1, lambda: pass_xy(1, 0))
-    step(2, lambda: pass_z(1, 2))
-    step(3, lambda: pass_xy(1, 1), lambda: pass_z(1, 3))
-    step(4, lambda: pass_d(1, 0))
-    step(5, lambda: pass_xy(1, 2))
-    step(6)
-    step(7, lambda: pass_xy(1, 3))
-
+        for c in loads[p]:
+            c.wait()
+        d = contract(w4[p], buf[0, p])
+        if p == 0:
+            acc[...] = d
+        else:
+            acc[...] += d
 
     def back(p):
         ready_sib(1, p)
@@ -206,9 +172,45 @@
         else:
             accb[...] += d
 
-    back(0)
-    pass_d(1, 1)
-    for p in (1, 2, 3, 4, 5, 6, 7):
+    for c in inputs:
+        c.wait()
+    pl.semaphore_wait(barrier, len(partners))
+
+    zcopy(0, 1).start()
+    across(0, 0)
+    zcopy(1, 1).start()
+    zcopy(0, 2).start()
+    zcopy(0, 3).start()
+    pass_z(0, 1)
+    pass_xy(0, 0)
+    across(1, 0)
+    pass_z(1, 1)
+    pass_z(0, 2)
+    zcopy(1, 2).start()
+    pass_xy(0, 1)
+    pass_d(0, 0)
+    pass_z(0, 3)
+    zcopy(1, 3).start()
+    pass_xy(0, 2)
+    pass_z(1, 2)
+    pass_xy(0, 3)
+    step(0)
+    pass_z(1, 3)
+    pass_d(0, 1)
+    step(4)
+    step(1)
+    sib(1, 0)
+    sib(2, 0)
+    step(2)
+    sib(3, 0)
+    step(5)
+    step(6)
+    sib(1, 1)
+    sib(2, 1)
+    step(3)
+    sib(3, 1)
+    step(7)
+    for p in (0, 4, 1, 2, 5, 6, 3, 7):
         back(p)
 
     chunk = hidden // 4
@@ -231,8 +233,11 @@
         for i in range(4):
             xcopy(t, i).wait_send()
             ycopy(t, i).wait_send()
-            dxcopy(t, i).wait_send()
-            dycopy(t, i).wait_send()
+            if t == 0:
+                dxcopy(t, i).wait_send()
+                dycopy(t, i).wait_send()
+            else:
+                dcopy(i).wait_send()
         for p in range(4):
             for h in (0, 1):
                 scopy(t, p, h).wait_send()
@@ -285,7 +290,7 @@
         out_shape=(jax.ShapeDtypeStruct((hidden, width), jnp.float32),) * 2,
         in_specs=[whole, whole, pl.BlockSpec((1, total, cols), lambda j: (j, 0, 0))],
         out_specs=(out, out),
-        compiler_params=pltpu.CompilerParams(vmem_limit_bytes=32 * 2**20),
+        compiler_params=pltpu.CompilerParams(vmem_limit_bytes=60 * 2**20),
         cost_estimate=pl.CostEstimate(
             flops=4 * hidden * width * total, bytes_accessed=8 * hidden * width,
             transcendentals=0),

time: 59.8 us -> 65 us (1.087)
  Pallas kernels: 55.5 us -> 64.2 us
  local copies, waits for them, and re-layouts: 3.39 us -> 0 us
    pallas_call x1, Pallas kernels: 44.2 us -> 51.8 us  [local_kernels(): pl.pallas_call(gather_kernel, out_shape=(jax.ShapeDtypeStruct((hidden, to...]
    unnamed x6 -> x0, local copies, waits for them, and re-layouts: 3.39 us -> none
    pallas_call x1, Pallas kernels: 11.3 us -> 12.4 us  [local_kernels(): pl.pallas_call(functools.partial(outer_kernel, scale), grid=(n_fs,), out_...]
where the time goes in v2:
time: 65 us; the launch traced here: 64.8 us
  Pallas kernels  64.2 us (99%)
    pallas_call x1, Pallas kernels, local_kernels(): pl.pallas_call(gather_kernel, out_shape=(jax.ShapeDtypeStruct((hidden, to...  51.8 us
    pallas_call x1, Pallas kernels, local_kernels(): pl.pallas_call(functools.partial(outer_kernel, scale), grid=(n_fs,), out_...  12.4 us

profile of v2, /device:TPU:0, one launch (start us, length us, event | category | flops | bytes accessed | tf_op | source)
XLA Modules:
  0.0 64.8 jit_solution(9656761881882423879)
XLA Ops:
  0.6 51.8 %gather_factors.1 = (bf16[512,128]{1,0:T(8,128)(2,1)}, bf16[512,128]{1,0:T(8,128)(2,1)}, bf16[8,128,1024]{2,1,0:T(8,128)(2,1)}) custom-call(bf16[32,1024]{1,0:T(8,128)(2,1)} %tok_hbm.1, bf16[32,1024]{1,0:T(8,128)(2,1)} %cot_hbm.1, bf16[512,8192]{1,0:T(8,128)(2,1)} %wg.1, bf16[512,8192]{1,0:T(8,128)(2,1)} %wu.1, bf16[512,8192]{1,0:T(8,128)(2,1)} %tg.1, ...), custom_call_target="tpu_custom_call" | custom-call | flops 5368709120 | bytes 41943040 | tf_op jit(solution)/shard_map/gather_factors/pallas_call | solution.py:261
  52.4 12.4 %outer.1 = (f32[512,8192]{1,0:T(8,128)}, f32[512,8192]{1,0:T(8,128)}) custom-call(bf16[512,128]{1,0:T(8,128)(2,1)} %get-tuple-element.5.fg, bf16[512,128]{1,0:T(8,128)(2,1)} %get-tuple-element.6.fu, bf16[8,128,1024]{2,1,0:T(8,128)(2,1)} %get-tuple-element.7.tok), custom_call_target="tpu_custom_call" | custom-call | flops 2147483648 | bytes 33554432 | tf_op jit(solution)/shard_map/outer/pallas_call | solution.py:287

commit v3 on v2

--- a/solution.py
+++ b/solution.py
@@ -48,7 +48,6 @@
 
     fx = feat(y, 1 - x, core)
     fy = feat(1 - y, x, core)
-    fd = feat(1 - y, 1 - x, core)
     fs = feat(y, x, 1 - core)
     fidx = [feat(yy, xx, cc) for cc in (core, 1 - core)
             for yy, xx in ((y, x), (y, 1 - x), (1 - y, x), (1 - y, 1 - x))]
@@ -60,7 +59,7 @@
         c.start()
 
     barrier = pltpu.get_barrier_semaphore()
-    partners = [(zi[1], f), (zi[2], f), (zi[3], f), (z, fx), (z, fy), (z, fd), (z, fs)]
+    partners = [(zi[1], f), (zi[2], f), (zi[3], f), (z, fx), (z, fy), (z, fs)]
     for who in partners:
         pl.semaphore_signal(barrier, inc=1, device_id=who, device_id_type=MESH)
 
@@ -105,29 +104,20 @@
         r = i * rows + half
         return remote(t, 2, 3, r, r, half, dxs.at[t, i], dxr.at[t, i], (z, fx))
 
-    def dcopy(i):
-        return remote(1, 0, 3, i * rows, i * rows, rows, dxs.at[1, i], dxr.at[1, i], (z, fd))
-
     def scopy(t, p, h):
         r = h * 2 * rows
         return remote(t, p, 4 + p, r, r, 2 * rows, ss.at[t, p, h], sr.at[t, p, h], (z, fs))
 
-    def across(t, i):
+    def own_xy(t):
+        xcopy(t, 0).start()
+        ycopy(t, 0).start()
+
+    def pass_z(t, i):
+        zcopy(t, i).wait_recv()
         xcopy(t, i).start()
         ycopy(t, i).start()
-        if t == 1:
-            dcopy(i).start()
-
-    def pass_z(t, i):
-        zcopy(t, i).wait_recv()
-        across(t, i)
         if i % 2 == 1:
             scopy(t, 0, i // 2).start()
-
-    def sib(p, h):
-        for i in (2 * h, 2 * h + 1):
-            {1: lambda: xcopy(1, i), 2: lambda: ycopy(1, i), 3: lambda: dcopy(i)}[p]().wait_recv()
-        scopy(1, p, h).start()
 
     def pass_xy(t, i):
         xcopy(t, i).wait_recv()
@@ -157,11 +147,16 @@
         out_copies[p].start()
         for c in loads[p]:
             c.wait()
-        d = contract(w4[p], buf[0, p])
-        if p == 0:
-            acc[...] = d
-        else:
-            acc[...] += d
+
+        def body(k, carry):
+            r = pl.ds(pl.multiple_of(k * hidden, hidden), hidden)
+            d = contract(w4[p, r], buf[0, p])
+            if p == 0:
+                acc[r] = d
+            else:
+                acc[r] += d
+            return carry
+        lax.fori_loop(0, 4, body, 0)
 
     def back(p):
         ready_sib(1, p)
@@ -177,40 +172,40 @@
     pl.semaphore_wait(barrier, len(partners))
 
     zcopy(0, 1).start()
-    across(0, 0)
+    own_xy(0)
     zcopy(1, 1).start()
+    own_xy(1)
     zcopy(0, 2).start()
     zcopy(0, 3).start()
     pass_z(0, 1)
     pass_xy(0, 0)
-    across(1, 0)
     pass_z(1, 1)
+    pass_xy(1, 0)
     pass_z(0, 2)
     zcopy(1, 2).start()
     pass_xy(0, 1)
-    pass_d(0, 0)
     pass_z(0, 3)
     zcopy(1, 3).start()
+    pass_d(0, 0)
+    pass_xy(1, 1)
+    step(0)
+    pass_z(1, 2)
     pass_xy(0, 2)
-    pass_z(1, 2)
+    pass_d(1, 0)
+    step(4)
+    pass_z(1, 3)
     pass_xy(0, 3)
-    step(0)
-    pass_z(1, 3)
+    step(1)
+    pass_xy(1, 2)
+    step(2)
     pass_d(0, 1)
-    step(4)
-    step(1)
-    sib(1, 0)
-    sib(2, 0)
-    step(2)
-    sib(3, 0)
     step(5)
+    pass_xy(1, 3)
     step(6)
-    sib(1, 1)
-    sib(2, 1)
     step(3)
-    sib(3, 1)
+    pass_d(1, 1)
     step(7)
-    for p in (0, 4, 1, 2, 5, 6, 3, 7):
+    for p in order:
         back(p)
 
     chunk = hidden // 4
@@ -233,11 +228,8 @@
         for i in range(4):
             xcopy(t, i).wait_send()
             ycopy(t, i).wait_send()
-            if t == 0:
-                dxcopy(t, i).wait_send()
-                dycopy(t, i).wait_send()
-            else:
-                dcopy(i).wait_send()
+            dxcopy(t, i).wait_send()
+            dycopy(t, i).wait_send()
         for p in range(4):
             for h in (0, 1):
                 scopy(t, p, h).wait_send()

time: 65 us -> 54.9 us (0.84)
  Pallas kernels: 64.2 us -> 54.1 us
    pallas_call x1, Pallas kernels: 51.8 us -> 41.7 us  [local_kernels(): pl.pallas_call(gather_kernel, out_shape=(jax.ShapeDtypeStruct((hidden, to...]
where the time goes in v3:
time: 54.9 us; the launch traced here: 54.8 us
  Pallas kernels  54.1 us (99%)
  between operations  0.64 us (1%)
    pallas_call x1, Pallas kernels, local_kernels(): pl.pallas_call(gather_kernel, out_shape=(jax.ShapeDtypeStruct((hidden, to...  41.7 us
    pallas_call x1, Pallas kernels, local_kernels(): pl.pallas_call(functools.partial(outer_kernel, scale), grid=(n_fs,), out_...  12.4 us

profile of v3, /device:TPU:0, one launch (start us, length us, event | category | flops | bytes accessed | tf_op | source)
XLA Modules:
  0.0 54.8 jit_solution(15341785354895406954)
XLA Ops:
  0.6 41.7 %gather_factors.1 = (bf16[512,128]{1,0:T(8,128)(2,1)}, bf16[512,128]{1,0:T(8,128)(2,1)}, bf16[8,128,1024]{2,1,0:T(8,128)(2,1)}) custom-call(bf16[32,1024]{1,0:T(8,128)(2,1)} %tok_hbm.1, bf16[32,1024]{1,0:T(8,128)(2,1)} %cot_hbm.1, bf16[512,8192]{1,0:T(8,128)(2,1)} %wg.1, bf16[512,8192]{1,0:T(8,128)(2,1)} %wu.1, bf16[512,8192]{1,0:T(8,128)(2,1)} %tg.1, ...), custom_call_target="tpu_custom_call" | custom-call | flops 5368709120 | bytes 41943040 | tf_op jit(solution)/shard_map/gather_factors/pallas_call | solution.py:253
  42.4 12.4 %outer.1 = (f32[512,8192]{1,0:T(8,128)}, f32[512,8192]{1,0:T(8,128)}) custom-call(bf16[512,128]{1,0:T(8,128)(2,1)} %get-tuple-element.5.fg, bf16[512,128]{1,0:T(8,128)(2,1)} %get-tuple-element.6.fu, bf16[8,128,1024]{2,1,0:T(8,128)(2,1)} %get-tuple-element.7.tok), custom_call_target="tpu_custom_call" | custom-call | flops 2147483648 | bytes 33554432 | tf_op jit(solution)/shard_map/outer/pallas_call | solution.py:279
